TPU v7x, 1024 devices: a whole 4x8x16 slice. The times are simulated.
1024 devices in a mesh: dp: 16 (over x, z_hi, core), expert: 64 (over y, z_lo).
Axes of the slice: x: 4, y: 8, z: 16 (z_hi: 2, z_lo: 8; z = z_hi * 8 + z_lo), core: 2. Of those that a mesh axis runs over, the one named last changes fastest.
Arguments:
- tokens: bfloat16 [16384, 4096], P('expert'), may hold values from -6 to 6
- expert_ids: int32 [16384, 8], P('expert'), may hold values from 0 to 255, as said below
- combine_weight: float32 [16384, 8], P('expert'), may hold values from 0.1 to 1
- old_plan: int32 [64], replicated, may hold values from 0 to 255, as said below
- new_plan: int32 [64], replicated, may hold values from 0 to 255, as said below
- gate_weight: bfloat16 [64, 4096, 2048], P('expert', None, 'dp'), may hold values from -0.09375 to 0.09375
- up_weight: bfloat16 [64, 4096, 2048], P('expert', None, 'dp'), may hold values from -0.09375 to 0.09375
- down_weight: bfloat16 [64, 2048, 4096], P('expert', 'dp'), may hold values from -0.125 to 0.125
- shared_gate: bfloat16 [4096, 2048], P(None, 'dp'), may hold values from -0.09375 to 0.09375
- shared_up: bfloat16 [4096, 2048], P(None, 'dp'), may hold values from -0.09375 to 0.09375
- shared_down: bfloat16 [2048, 4096], P('dp'), may hold values from -0.125 to 0.125
Outputs:
- mixed_out: bfloat16 [16384, 4096], P('expert', 'dp')
Inputs may be any that keep to these rules, and one draw needn't show every extreme that they name: `old_plan`: the 64 experts are different. `new_plan`: slot s holds old_plan[s] or old_plan[s - 1] (slot 0 may take from slot 63); slots 0, 32 and 63 change; apart from slots 0 and 63, two neighbouring slots never both change. `expert_ids`: the 8 experts of a token are different; the tokens of one device send at most 2 kept routes to the slots of one expert together, and some slot gets exactly 2 from the tokens of every device.
All inputs are finite; a program needn't handle non-finite values.
Results may differ from a plain program's by a relative error of at most 0.014.
Values may be sent and summed in bfloat16 or wider, within the bound.
A program may use at most 64 MiB of HBM per device.

v0:
```python
import jax
import jax.numpy as jnp
from jax import lax
from jax.sharding import PartitionSpec as P

CAP = 2


def from_behind(value, axis, steps):
    count = lax.axis_size(axis)
    pairs = [(source, (source + steps) % count) for source in range(count)]
    return lax.ppermute(value, axis, pairs)


def route_slots(expert_ids, token_index, new_plan):
    matches = (expert_ids[:, :, None] == new_plan[None, None, :]).astype(jnp.int32)
    counted = jnp.sum(matches, axis=2, keepdims=True)
    before = jnp.cumsum(matches, axis=2) - matches
    wanted = jnp.remainder(token_index[:, None, None], jnp.maximum(counted, 1))
    return matches * (before == wanted).astype(jnp.int32)


def expert_block(row_block, gate_part, up_part, down_part):
    gate_value = jnp.dot(row_block, gate_part, preferred_element_type=jnp.float32)
    up_value = jnp.dot(row_block, up_part, preferred_element_type=jnp.float32)
    hidden = (jax.nn.silu(gate_value) * up_value).astype(jnp.bfloat16)
    return jnp.dot(hidden, down_part, preferred_element_type=jnp.float32).astype(jnp.bfloat16)


def combine_routes(rows, row_index, route_scale):
    total = jnp.zeros((row_index.shape[0], rows.shape[1]), jnp.float32)
    for route in range(row_index.shape[1]):
        picked = rows[row_index[:, route]].astype(jnp.float32)
        total = total + route_scale[:, route][:, None] * picked
    return total


def local(
    tokens,
    expert_ids,
    combine_weight,
    old_plan,
    new_plan,
    gate_weight,
    up_weight,
    down_weight,
    shared_gate,
    shared_up,
    shared_down,
):
    slot_count = lax.axis_size("expert")
    own_index = lax.axis_index("expert")
    tok_rows = tokens.shape[0]
    route_count = expert_ids.shape[1]
    model_width = tokens.shape[1]
    token_index = own_index * tok_rows + jnp.arange(tok_rows, dtype=jnp.int32)
    chosen = route_slots(expert_ids, token_index, new_plan)
    changed = (new_plan != old_plan).astype(jnp.int32)
    gate_now = gate_weight[0]
    up_now = up_weight[0]
    down_now = down_weight[0]
    capacity = CAP
    bundle = jnp.concatenate((gate_now, up_now, down_now.reshape(gate_now.shape)), axis=0)
    arrived_weights = from_behind(bundle, "expert", 1)
    bundle = jnp.where(changed[own_index] > 0, arrived_weights, bundle)
    gate_now = bundle[:model_width]
    up_now = bundle[model_width : 2 * model_width]
    down_now = bundle[2 * model_width :].reshape(down_now.shape)
    flat_targets = chosen.reshape(tok_rows * route_count, slot_count)
    earlier = jnp.cumsum(flat_targets, axis=0) - flat_targets
    position = jnp.sum(earlier * flat_targets, axis=1).reshape(tok_rows, route_count)
    columns = lax.broadcasted_iota(jnp.int32, (1, 1, 1, capacity), 3)
    placed = chosen[:, :, :, None] * (position[:, :, None, None] == columns).astype(jnp.int32)
    routing = jnp.sum(placed, axis=1).reshape(tok_rows, slot_count * capacity)
    slot_numbers = lax.broadcasted_iota(jnp.int32, (1, 1, slot_count), 2)
    slot_of = jnp.sum(chosen * slot_numbers, axis=2)
    kept = jnp.sum(chosen, axis=2)
    row_index = slot_of * capacity + position * kept
    route_scale = combine_weight * kept.astype(jnp.float32)
    outgoing = lax.dot_general(
        routing.astype(jnp.bfloat16),
        tokens,
        (((0,), (0,)), ((), ())),
        preferred_element_type=jnp.float32,
    )
    outgoing = outgoing.astype(jnp.bfloat16).reshape(slot_count, capacity, model_width)
    arrived = lax.all_to_all(outgoing, "expert", split_axis=0, concat_axis=0, tiled=True)
    senders, item_count, features = arrived.shape
    result = expert_block(
        arrived.reshape(senders * item_count, features), gate_now, up_now, down_now
    )
    slot_part = result.reshape(senders, item_count, features)
    shared_part = expert_block(tokens, shared_gate, shared_up, shared_down)
    slot_rows = slot_part.reshape(slot_count * capacity, model_width).astype(jnp.float32)
    slot_sum, shared_sum = (
        lax.psum_scatter(
            slot_rows.astype(jnp.bfloat16), "dp", scatter_dimension=1, tiled=True
        ).astype(jnp.float32),
        lax.psum_scatter(
            shared_part.astype(jnp.float32).astype(jnp.bfloat16),
            "dp",
            scatter_dimension=1,
            tiled=True,
        ).astype(jnp.float32),
    )
    returned = lax.all_to_all(
        slot_sum.reshape(slot_count, capacity, slot_sum.shape[1]).astype(jnp.bfloat16),
        "expert",
        split_axis=0,
        concat_axis=0,
        tiled=True,
    ).astype(jnp.float32)
    routed = combine_routes(
        returned.reshape(slot_count * capacity, returned.shape[2]), row_index, route_scale
    )
    mixed_out = (shared_sum + routed).astype(jnp.bfloat16)
    return mixed_out


def solution(mesh):
    in_specs = (
        P("expert", None),
        P("expert", None),
        P("expert", None),
        P(),
        P(),
        P("expert", None, "dp"),
        P("expert", None, "dp"),
        P("expert", "dp", None),
        P(None, "dp"),
        P(None, "dp"),
        P("dp", None),
    )
    out_specs = P("expert", "dp")
    return jax.shard_map(local, mesh=mesh, in_specs=in_specs, out_specs=out_specs, check_vma=False)
```

profile of v0, /device:TPU:1, one launch (start us, length us, event | category | flops | bytes accessed | tf_op | source)
XLA Modules:
  0.0 416.9 jit_solution(15213930785191100931)
XLA Ops:
  6.5 1.7 reshape_squeeze.3
  8.3 0.0 copy-start.6
  8.3 10.1 %pad_maximum_fusion = bf16[12288,128]{1,0:T(8,128)(2,1)} fusion(bf16[4096,128]{1,0:T(8,128)(2,1)S(1)} %reshape_squeeze.3, bf16[4096,128]{1,0:T(8,128)(2,1)} %bitcast.48, bf16[4096,128]{1,0:T(8,128)(2,1)} %bitcast.50), kind=kLoop, calls=%fused_computation.11 | loop fusion | flops 9437184 | bytes 6291456 | tf_op jit(solution)/shard_map/concatenate | solution.py:63
  18.4 4.8 %collective-permute-start = (bf16[12288,128]{1,0:T(8,128)(2,1)}, bf16[12288,128]{1,0:T(8,128)(2,1)}, u32[]{:S(2)}, u32[]{:S(2)}) collective-permute-start(bf16[12288,128]{1,0:T(8,128)(2,1)} %pad_maximum_fusion), channel_id=1, source_target_pairs={{0,1},{1,2},{2,3},{3,4},{4,5},{5,6},{6,7},{7,8},{8,9},{9,10},{10,1... | collective-permute-start | bytes 9437192 | tf_op jit(solution)/shard_map/ppermute | solution.py:12
  23.3 0.1 convert_reduce_fusion
  23.4 0.1 add_select_fusion.1
  23.5 1.3 multiply_reduce_fusion.1
  24.8 0.1 copy.44
  24.9 1.5 copy.43
  26.4 0.1 rem.22.clone
  26.5 0.1 rem.24
  26.6 0.1 copy.46
  26.8 0.1 max.19
  26.9 0.1 eq.81
  27.0 0.1 add_select_fusion
  27.1 2.4 convert_select_fusion
  29.5 2.4 copy.47
  31.8 34.5 %reduce-window.6 = s32[64,16,128]{2,1,0:T(8,128)} reduce-window(s32[64,16,128]{2,1,0:T(8,128)} %copy.47, s32[]{:T(128)} %constant.17.clone.1), window={size=1x1x128 pad=0_0x0_0x127_0}, to_apply=%region_4.5 | reduce-window | flops 16646144 | bytes 1048580 | tf_op jit(solution)/shard_map/reduce-window
  66.3 2.0 slice.101
  68.4 1.5 copy.54
  69.8 0.2 reduce-window.9
  70.0 2.1 broadcast_add_fusion
  72.1 2.4 copy.55
  74.5 2.0 fusion.4
  76.5 0.1 eq.88
  76.7 0.1 copy.51
  76.7 1.2 copy.42
  78.0 0.1 multiply_reduce_fusion
  78.1 0.1 copy.52
  78.2 0.0 copy-start.11
  78.2 1.4 convolution_convert_fusion.2
  79.6 2.6 reshape.102
  82.2 20.2 %all-to-all-start = ((bf16[64,2,4096]{2,1,0:T(2,128)(2,1)}), bf16[64,2,4096]{2,1,0:T(2,128)(2,1)}, u32[]{:S(2)}, u32[]{:S(2)}) async-start(bf16[64,2,4096]{2,1,0:T(2,128)(2,1)} %reshape.102), calls=%async_computation.1 | async-start | bytes 2097152 | tf_op jit(solution)/shard_map/all_to_all | solution.py:87
  102.4 0.2 reduce-scatter.5.cloned.1.call-start
  102.7 0.6 dynamic_slice.3
  103.9 9.1 %broadcast_select_fusion = bf16[12288,128]{1,0:T(8,128)(2,1)S(1)} fusion(bf16[12288,128]{1,0:T(8,128)(2,1)} %collective-permute-done, pred[]{:T(512)} %bitcast.8, bf16[4096,128]{1,0:T(8,128)(2,1)S(1)} %copy-done.2, bf16[4096,128]{1,0:T(8,128)(2,1)} %bitcast.49, bf16[4096,128]{1,0:T(8,128)(2,1)} %bitcast.51), kind=kLoop, calls=%fused_computation.12 | loop fusion | flops 11010048 | bytes 9437185 | tf_op jit(solution)/shard_map/jit(_where)/select_n | solution.py:65
  113.0 1.7 copy-done.3
  114.7 0.1 slice.105
  114.7 1.3 reshape.104
  116.0 37.5 %all-to-all-done = bf16[64,2,4096]{2,1,0:T(2,128)(2,1)} async-done(((bf16[64,2,4096]{2,1,0:T(2,128)(2,1)}), bf16[64,2,4096]{2,1,0:T(2,128)(2,1)}, u32[]{:S(2)}, u32[]{:S(2)}) %all-to-all-start) | async-done | bytes 1048608 | tf_op jit(solution)/shard_map/all_to_all | solution.py:87
  153.5 2.3 reshape.103
  155.8 2.0 fusion.5
  157.8 3.3 convolution_convert_fusion.1
  161.1 0.0 reduce-scatter.5.cloned.1.call-update
  161.1 0.0 reduce-scatter.3.cloned.1.call-start
  161.2 2.0 fusion.28
  163.2 0.0 copy-start.8
  163.2 3.9 convolution_convert_fusion
  167.1 0.0 reduce-scatter.3.cloned.1.call-update
  167.3 110.7 %reduce-scatter.5.cloned.1.call-done = bf16[128,256]{1,0:T(8,128)(2,1)} async-done(((bf16[128,4096]{1,0:T(8,128)(2,1)}), bf16[128,256]{1,0:T(8,128)(2,1)}) %reduce-scatter.5.cloned.1.call-update) | async-done | bytes 65552 | tf_op jit(solution)/shard_map/reduce_scatter | solution.py:96
  277.9 1.5 convert_element_type.75
  279.4 7.7 %all-to-all-start.1 = ((bf16[64,2,256]{2,1,0:T(2,128)(2,1)}), bf16[64,2,256]{2,1,0:T(2,128)(2,1)S(1)}, u32[]{:S(2)}, u32[]{:S(2)}) async-start(bf16[64,2,256]{2,1,0:T(2,128)(2,1)} %convert_element_type.75), calls=%async_computation.3 | async-start | bytes 131072 | tf_op jit(solution)/shard_map/all_to_all | solution.py:106
  287.2 0.6 fusion.27
  287.8 12.8 %all-to-all-done.1 = bf16[64,2,256]{2,1,0:T(2,128)(2,1)S(1)} async-done(((bf16[64,2,256]{2,1,0:T(2,128)(2,1)}), bf16[64,2,256]{2,1,0:T(2,128)(2,1)S(1)}, u32[]{:S(2)}, u32[]{:S(2)}) %all-to-all-start.1) | async-done | bytes 65568 | tf_op jit(solution)/shard_map/all_to_all | solution.py:106
  300.6 1.0 gather_fusion.7
  301.5 1.0 gather_fusion.6
  302.5 1.0 gather_fusion.5
  303.5 1.0 gather_fusion.4
  304.5 1.0 gather_fusion.3
  305.4 1.7 gather_fusion.2
  307.1 1.7 gather_fusion.1
  308.8 1.7 gather_fusion
  310.5 97.4 %reduce-scatter.3.cloned.1.call-done = bf16[256,256]{1,0:T(8,128)(2,1)} async-done(((bf16[256,4096]{1,0:T(8,128)(2,1)}), bf16[256,256]{1,0:T(8,128)(2,1)}) %reduce-scatter.3.cloned.1.call-update) | async-done | bytes 131088 | tf_op jit(solution)/shard_map/reduce_scatter | solution.py:99
  407.9 2.2 add_convert_fusion
  (38 shorter events, 0.2 us)
Async XLA Ops:
  6.5 71.6 %copy-start = (bf16[256,4096]{1,0:T(8,128)(2,1)S(1)}, bf16[256,4096]{1,0:T(8,128)(2,1)}, u32[]{:S(2)}) copy-start(bf16[256,4096]{1,0:T(8,128)(2,1)} %param.11) | copy-start | bytes 6291460
  8.2 10.2 %copy-start.1 = (bf16[4096,128]{1,0:T(8,128)(2,1)}, bf16[4096,128]{1,0:T(8,128)(2,1)S(1)}, u32[]{:S(2)}) copy-start(bf16[4096,128]{1,0:T(8,128)(2,1)S(1)} %reshape_squeeze.3) | copy-start | bytes 3145732
  8.3 15.0 %copy-start.6 = (s32[256,8]{0,1:T(8,128)S(1)}, s32[256,8]{0,1:T(8,128)}, u32[]{:S(2)}) copy-start(s32[256,8]{0,1:T(8,128)} %param.12) | copy-start | bytes 24580
  8.3 15.0 %copy-start.7 = (s32[64]{0:T(128)S(1)}, s32[64]{0:T(128)}, u32[]{:S(2)}) copy-start(s32[64]{0:T(128)} %param.15) | copy-start | bytes 772
  18.4 85.5 %collective-permute-start = (bf16[12288,128]{1,0:T(8,128)(2,1)}, bf16[12288,128]{1,0:T(8,128)(2,1)}, u32[]{:S(2)}, u32[]{:S(2)}) collective-permute-start(bf16[12288,128]{1,0:T(8,128)(2,1)} %pad_maximum_fusion), channel_id=1, source_target_pairs={{0,1},{1,2},{2,3},{3,4},{4,5},{5,6},{6,7},{7,8},{8,9},{9,10},{10,1... | collective-permute-start | bytes 9437192 | tf_op jit(solution)/shard_map/ppermute | solution.py:12
  78.2 24.4 %copy-start.11 = (s32[64]{0:T(128)S(1)}, s32[64]{0:T(128)}, u32[]{:S(2)}) copy-start(s32[64]{0:T(128)} %param.14) | copy-start | bytes 772
  78.2 25.7 %copy-start.2 = (bf16[4096,128]{1,0:T(8,128)(2,1)S(1)}, bf16[4096,128]{1,0:T(8,128)(2,1)}, u32[]{:S(2)}) copy-start(bf16[4096,128]{1,0:T(8,128)(2,1)} %copy-done.1) | copy-start | bytes 3145732
  82.2 71.3 %all-to-all-start = ((bf16[64,2,4096]{2,1,0:T(2,128)(2,1)}), bf16[64,2,4096]{2,1,0:T(2,128)(2,1)}, u32[]{:S(2)}, u32[]{:S(2)}) async-start(bf16[64,2,4096]{2,1,0:T(2,128)(2,1)} %reshape.102), calls=%async_computation.1 | async-start | bytes 2097152 | tf_op jit(solution)/shard_map/all_to_all | solution.py:87
  102.4 175.5 %reduce-scatter.5.cloned.1.call-start = ((), (), s32[]{:S(2)}) async-start(), calls=%async_computation.5 | async-start | bytes 1114112 | tf_op jit(solution)/shard_map/reduce_scatter | solution.py:96
  113.0 1.7 copy-start.3
  116.0 41.7 %copy-start.4 = (bf16[128,4096]{1,0:T(8,128)(2,1)S(1)}, bf16[128,4096]{1,0:T(8,128)(2,1)}, u32[]{:S(2)}) copy-start(bf16[128,4096]{1,0:T(8,128)(2,1)} %reshape.104) | copy-start | bytes 3145732
  161.1 2.1 copy-start.5
  161.1 246.8 %reduce-scatter.3.cloned.1.call-start = ((), (), s32[]{:S(2)}) async-start(), calls=%async_computation.4 | async-start | bytes 2228224 | tf_op jit(solution)/shard_map/reduce_scatter | solution.py:99
  163.2 4.1 copy-start.8
  279.4 21.1 %all-to-all-start.1 = ((bf16[64,2,256]{2,1,0:T(2,128)(2,1)}), bf16[64,2,256]{2,1,0:T(2,128)(2,1)S(1)}, u32[]{:S(2)}, u32[]{:S(2)}) async-start(bf16[64,2,256]{2,1,0:T(2,128)(2,1)} %convert_element_type.75), calls=%async_computation.3 | async-start | bytes 131072 | tf_op jit(solution)/shard_map/all_to_all | solution.py:106
  305.4 102.5 %copy-start.9 = (f32[256,1]{0,1:T(1,128)S(1)}, f32[256,1]{0,1:T(1,128)}, u32[]{:S(2)}) copy-start(f32[256,1]{0,1:T(1,128)} %get-tuple-element.8) | copy-start | bytes 3076
  307.1 100.8 %copy-start.10 = (f32[256,1]{0,1:T(1,128)S(1)}, f32[256,1]{0,1:T(1,128)}, u32[]{:S(2)}) copy-start(f32[256,1]{0,1:T(1,128)} %get-tuple-element.9) | copy-start | bytes 3076
Sparse Core Ops, SparseCore 0:
  161.3 116.6 reduce-scatter.4
  284.9 122.9 reduce-scatter.2
where the time goes:
time: 421 us; the launch traced here: 417 us
  waiting for transfers between devices  258 us (61%)
  other arithmetic  64.4 us (15%)
  local copies, waits for them, and re-layouts  34 us (8%)
  starting transfers between devices  32.9 us (8%)
  between operations  14.5 us (3%)
  matrix products  12.6 us (3%)
    reduce_scatter x1, waiting for transfers between devices, local(): lax.psum_scatter(slot_rows.astype(jnp.bfloat16), 'dp', scatter_dimension=...  111 us
    reduce_scatter x1, waiting for transfers between devices, local(): lax.psum_scatter(shared_part.astype(jnp.float32).astype(jnp.bfloat16), 'd...  97.4 us
    all_to_all x1, waiting for transfers between devices, local(): lax.all_to_all(outgoing, 'expert', split_axis=0, concat_axis=0, tiled=True)  37.5 us
    another operation x3, other arithmetic  36.8 us
    all_to_all x1, starting transfers between devices, local(): lax.all_to_all(outgoing, 'expert', split_axis=0, concat_axis=0, tiled=True)  20.2 us
    all_to_all x1, waiting for transfers between devices, local(): lax.all_to_all(slot_sum.reshape(slot_count, capacity, slot_sum.shape[1])....  12.8 us
    concatenate x1, other arithmetic, local(): jnp.concatenate((gate_now, up_now, down_now.reshape(gate_now.shape)), axi...  10.1 us
    gather x8, local copies, waits for them, and re-layouts, combine_routes(): picked = rows[row_index[:, route]].astype(jnp.float32)  9.86 us
  transfers between devices with their start and end apart: 5, of which 4 were waited for; matrix products, arithmetic and copies ran while one was open for 21% of the time, Pallas kernels for 0%

commit v1 on v0

v1 whole, which is shorter than its diff:
```python
import jax
import jax.numpy as jnp
from jax import lax
from jax.experimental import pallas as pl
from jax.experimental.pallas import tpu as pltpu
from jax.sharding import PartitionSpec as P

MESH = pl.DeviceIdType.MESH
BF16 = jnp.bfloat16
F32 = jnp.float32

NX, NY, NZ, NL = 4, 8, 16, 8
TOK = 256
D = 4096
HB = 128
SLOTS = 64
ROWS = 128
CH = 512
FB = 256


def dot(a, b):
    return jnp.dot(a, b, preferred_element_type=F32)


def gated(g, u):
    return (g / (1.0 + jnp.exp(-g)) * u).astype(BF16)


def kernel(
    tokens_in, ids_in, cw_in, old_in, new_in, gate_in, up_in, down_in, sgate_in, sup_in, sdown_in,
    out_ref,
    tokens, ids, cw, old, new, wgu, swgu, down, sdown,
    gbuf, abuf, bbuf, xrows, hid, shid,
    s_send, s_recv, s_mid, s_own, z_send, z_mid, z_recv,
    p_own, p_send, p_recv, p_mid, rbuf, dbuf, ysend, ebuf, wcomb,
    lsem, y_ss, y_rs, z_ss, z_rs, a_ss, a_rs, b_ss, b_rs, x_ss, x_rs, r_ss, r_rs, v_ss, v_rs,
    t_ss, t_rs, u_ss, u_rs,
):
    d = lax.axis_index("dp")
    e = lax.axis_index("expert")
    x = lax.div(d, 4)
    zh = lax.rem(lax.div(d, 2), 2)
    c = lax.rem(d, 2)
    y = lax.div(e, NL)
    zl = lax.rem(e, NL)
    z = zh * NL + zl
    xa = x + 1 - 2 * lax.rem(x, 2)
    xb = 3 - x
    xo = lax.rem(x + 2, NX)
    oc = 1 - c

    def dev(x_, y_, z_, c_):
        return (x_ * 4 + lax.div(z_, NL) * 2 + c_, y_ * NL + lax.rem(z_, NL))

    sib = dev(x, y, z, oc)
    dev_a = dev(xa, y, z, c)
    dev_b = dev(xb, y, z, c)

    def load(src, dst, i):
        copy = pltpu.make_async_copy(src, dst, lsem.at[i])
        copy.start()
        return copy

    l_old = load(old_in, old, 0)
    l_new = load(new_in, new, 1)
    l_ids = load(ids_in, ids, 2)
    l_cw = load(cw_in, cw, 3)
    l_tok = load(tokens_in, tokens, 4)
    l_sg = load(sgate_in, swgu.at[:, pl.ds(0, HB)], 5)
    l_su = load(sup_in, swgu.at[:, pl.ds(HB, HB)], 6)
    l_sd = load(sdown_in, sdown.at[c], 7)
    l_g = load(gate_in.at[0], wgu.at[:, pl.ds(0, HB)], 8)
    l_u = load(up_in.at[0], wgu.at[:, pl.ds(HB, HB)], 9)
    l_d = load(down_in.at[0], down.at[c], 10)

    barrier = pltpu.get_barrier_semaphore()
    peers = [sib, dev_a, dev_b]
    peers += [dev(x, lax.rem(y + r, NY), z, c) for r in range(1, NY)]
    peers += [dev(x, y, lax.rem(z + r, NZ), c) for r in range(1, NZ)]
    for peer in peers:
        pl.semaphore_signal(barrier, inc=1, device_id=peer, device_id_type=MESH)

    sends = []

    def send(src, dst, ss, rs, peer):
        copy = pltpu.make_async_remote_copy(
            src_ref=src, dst_ref=dst, send_sem=ss, recv_sem=rs, device_id=peer, device_id_type=MESH
        )
        copy.start()
        sends.append(copy)

    def arrived(dst, ss, rs):
        pltpu.make_async_remote_copy(
            src_ref=dst, dst_ref=dst, send_sem=ss, recv_sem=rs, device_id=sib, device_id_type=MESH
        ).wait_recv()

    l_old.wait()
    l_new.wait()
    lane8 = lax.broadcasted_iota(jnp.int32, (8, ROWS), 1)
    slot8 = lax.div(lane8, 2)

    held = jnp.full((8, ROWS), -1, jnp.int32)
    for s in range(SLOTS):
        held = jnp.where(slot8 == s, old[s], held)
    kept = jnp.zeros((8, ROWS), jnp.bool_)
    for s in range(SLOTS):
        kept = kept | (held == new[s])
    held = jnp.where(kept, held, -1).astype(F32)[0:1, :]
    held = jnp.transpose(jnp.broadcast_to(held, (ROWS, ROWS))).astype(jnp.int32)
    held = jnp.concatenate([held, held], axis=1)
    l_ids.wait()
    l_cw.wait()
    match = jnp.zeros((ROWS, TOK), F32)
    weight = jnp.zeros((ROWS, TOK), F32)
    for k in range(8):
        hit = ids[k : k + 1, :] == held
        match = match + jnp.where(hit, 1.0, 0.0)
        weight = weight + jnp.where(hit, cw[k : k + 1, :], 0.0)
    upper = jnp.where(
        lax.broadcasted_iota(jnp.int32, (TOK, TOK), 0) < lax.broadcasted_iota(jnp.int32, (TOK, TOK), 1),
        1.0, 0.0,
    ).astype(BF16)
    before = dot(match.astype(BF16), upper)
    place = lax.rem(lax.broadcasted_iota(jnp.int32, (ROWS, TOK), 0), 2).astype(F32)
    here = jnp.where(before == place, 1.0, 0.0)
    pick = (match * here).astype(BF16)
    weight = weight * here
    row = lax.broadcasted_iota(jnp.int32, (ROWS, ROWS), 0)
    col = lax.broadcasted_iota(jnp.int32, (ROWS, ROWS), 1)
    swapped = lax.rem(lax.div(row, 2), 8) * 16 + lax.div(row, 16) * 2 + lax.rem(row, 2)
    swap = jnp.where(col == swapped, 1.0, 0.0).astype(BF16)

    l_tok.wait()
    chunk = tokens[:, pl.ds(pl.multiple_of(x * 1024 + c * CH, CH), CH)]
    gbuf[...] = dot(pick, chunk).astype(BF16).reshape(NY, 16, CH)
    abuf[y] = gbuf[y]

    pl.semaphore_wait(barrier, len(peers))
    for r in range(1, NY):
        to = lax.rem(y + r, NY)
        send(gbuf.at[to], abuf.at[y], y_ss.at[r], y_rs.at[r], dev(x, to, z, c))
    send(sdown_in, sdown.at[c], a_ss.at[0], a_rs.at[0], sib)
    send(down_in.at[0], down.at[c], a_ss.at[1], a_rs.at[1], sib)

    weight = jnp.transpose(weight)
    high = weight.astype(BF16)
    wcomb[0] = high
    wcomb[1] = (weight - high.astype(F32)).astype(BF16)

    l_sg.wait()
    l_su.wait()
    both = dot(tokens[...], swgu[...])
    shid[c] = gated(both[:, :HB], both[:, HB:])
    send(shid.at[c], shid.at[c], a_ss.at[2], a_rs.at[2], sib)

    for r in range(1, NY):
        frm = lax.rem(y + NY - r, NY)
        arrived(abuf.at[frm], y_ss.at[r], y_rs.at[r])
    bbuf[...] = dot(swap, abuf[...].reshape(ROWS, CH)).astype(BF16).reshape(NL, 16, CH)
    steps = [1, 15, 2, 14, 3, 13, 4 + 8 * c]
    for i, step in enumerate(steps):
        to = lax.rem(z + step, NZ)
        send(bbuf.at[lax.rem(to, NL)], xrows.at[c, x, zl], z_ss.at[i], z_rs.at[i], dev(x, y, to, c))
    xrows[c, x, zl] = bbuf[zl]

    l_sd.wait()
    arrived(sdown.at[oc], a_ss.at[0], a_rs.at[0])
    arrived(shid.at[oc], a_ss.at[2], a_rs.at[2])
    sh0 = shid[0]
    sh1 = shid[1]

    def columns(ref, core, x_, half):
        at = pl.multiple_of(x_ * 1024 + half * CH + c * FB, FB)
        return ref[core, :, pl.ds(at, FB)]

    def shared_part(x_, half):
        return dot(sh0, columns(sdown, 0, x_, half)) + dot(sh1, columns(sdown, 1, x_, half))

    HR = TOK // 2
    for half in range(2):
        part = shared_part(xo, half).astype(BF16)
        s_send[0, half] = part[:HR]
        s_send[1, half] = part[HR:]
    send(s_send.at[0], s_recv.at[0], b_ss.at[0], b_rs.at[0], dev_a)
    send(s_send.at[1], s_recv.at[1], b_ss.at[1], b_rs.at[1], dev_b)
    for half in range(2):
        part = shared_part(xa, half)
        s_send[2, half] = part[:HR].astype(BF16)
        s_mid[0, half] = part[HR:]
        part = shared_part(xb, half)
        s_send[3, half] = part[HR:].astype(BF16)
        s_mid[1, half] = part[:HR]
    send(s_send.at[2], s_recv.at[2], b_ss.at[2], b_rs.at[2], dev_a)
    send(s_send.at[3], s_recv.at[3], b_ss.at[3], b_rs.at[3], dev_b)
    for half in range(2):
        s_own[half] = shared_part(x, half)

    for i, step in enumerate(steps):
        frm = lax.rem(z + NZ - step, NZ)
        arrived(xrows.at[c, x, lax.rem(frm, NL)], z_ss.at[i], z_rs.at[i])

    def rows_of(x_, half):
        return xrows.at[c, x_, pl.ds(half * 4, 4)]

    send(rows_of(x, 0), rows_of(x, 0), x_ss.at[0], x_rs.at[0], dev_a)
    send(rows_of(x, 1), rows_of(x, 1), x_ss.at[1], x_rs.at[1], dev_b)
    send(rows_of(x, 1), rows_of(x, 1), x_ss.at[2], x_rs.at[2], dev_a)
    send(rows_of(x, 0), rows_of(x, 0), x_ss.at[3], x_rs.at[3], dev_b)
    send(xrows.at[c, x], xrows.at[c, x], a_ss.at[3], a_rs.at[3], sib)

    l_g.wait()
    l_u.wait()

    def product(core, x_):
        at = pl.multiple_of(x_ * 1024 + core * CH, CH)
        return dot(xrows[core, x_].reshape(ROWS, CH), wgu[pl.ds(at, CH), :])

    acc = product(c, x)
    arrived(rows_of(xa, 0), x_ss.at[0], x_rs.at[0])
    send(rows_of(xa, 0), rows_of(xa, 0), x_ss.at[4], x_rs.at[4], dev_b)
    arrived(rows_of(xb, 1), x_ss.at[1], x_rs.at[1])
    send(rows_of(xb, 1), rows_of(xb, 1), x_ss.at[5], x_rs.at[5], dev_a)
    arrived(rows_of(xa, 1), x_ss.at[2], x_rs.at[2])
    send(xrows.at[c, xa], xrows.at[c, xa], a_ss.at[4], a_rs.at[4], sib)
    arrived(rows_of(xb, 0), x_ss.at[3], x_rs.at[3])
    send(xrows.at[c, xb], xrows.at[c, xb], a_ss.at[5], a_rs.at[5], sib)
    acc = acc + product(c, xa) + product(c, xb)

    arrived(s_recv.at[0], b_ss.at[0], b_rs.at[0])
    s_send[5] = (s_mid[1] + s_recv[0].astype(F32)).astype(BF16)
    send(s_send.at[5], s_recv.at[5], b_ss.at[5], b_rs.at[5], dev_b)
    arrived(s_recv.at[1], b_ss.at[1], b_rs.at[1])
    s_send[4] = (s_mid[0] + s_recv[1].astype(F32)).astype(BF16)
    send(s_send.at[4], s_recv.at[4], b_ss.at[4], b_rs.at[4], dev_a)

    arrived(rows_of(xo, 0), x_ss.at[4], x_rs.at[4])
    send(rows_of(xo, 0), rows_of(xo, 0), a_ss.at[6], a_rs.at[6], sib)
    arrived(rows_of(xo, 1), x_ss.at[5], x_rs.at[5])
    send(rows_of(xo, 1), rows_of(xo, 1), a_ss.at[7], a_rs.at[7], sib)
    acc = acc + product(c, xo)
    arrived(xrows.at[oc, x], a_ss.at[3], a_rs.at[3])
    acc = acc + product(oc, x)
    arrived(xrows.at[oc, xa], a_ss.at[4], a_rs.at[4])
    acc = acc + product(oc, xa)
    arrived(xrows.at[oc, xb], a_ss.at[5], a_rs.at[5])
    acc = acc + product(oc, xb)
    arrived(xrows.at[oc, xo, pl.ds(0, 4)], a_ss.at[6], a_rs.at[6])
    arrived(xrows.at[oc, xo, pl.ds(4, 4)], a_ss.at[7], a_rs.at[7])
    acc = acc + product(oc, xo)
    hid[c] = gated(acc[:, :HB], acc[:, HB:])
    send(hid.at[c], hid.at[c], a_ss.at[8], a_rs.at[8], sib)

    for i in range(2, 6):
        arrived(s_recv.at[i], b_ss.at[i], b_rs.at[i])
    first = s_own[:, :HR, :] + s_recv[2].astype(F32) + s_recv[5].astype(F32)
    second = s_own[:, HR:, :] + s_recv[3].astype(F32) + s_recv[4].astype(F32)
    s_own[:, :HR, :] = first
    s_own[:, HR:, :] = second
    z_send[...] = s_own[1 - zh].astype(BF16)
    dev_up = dev(x, y, lax.rem(z + 4, NZ), c)
    dev_dn = dev(x, y, lax.rem(z + 12, NZ), c)
    send(z_send.at[pl.ds(0, HR)], z_mid.at[pl.ds(0, HR)], t_ss.at[0], t_rs.at[0], dev_up)
    send(z_send.at[pl.ds(HR, HR)], z_mid.at[pl.ds(HR, HR)], t_ss.at[1], t_rs.at[1], dev_dn)

    l_d.wait()
    arrived(down.at[oc], a_ss.at[1], a_rs.at[1])
    arrived(hid.at[oc], a_ss.at[8], a_rs.at[8])
    h0 = hid[0]
    h1 = hid[1]

    def route_part(x_, half):
        return dot(h0, columns(down, 0, x_, half)) + dot(h1, columns(down, 1, x_, half))

    HP = ROWS // 2
    for half in range(2):
        part = route_part(xo, half).astype(BF16)
        p_send[0, half] = part[:HP]
        p_send[1, half] = part[HP:]
    send(p_send.at[0], p_recv.at[0], r_ss.at[0], r_rs.at[0], dev_a)
    send(p_send.at[1], p_recv.at[1], r_ss.at[1], r_rs.at[1], dev_b)
    for half in range(2):
        part = route_part(xa, half)
        p_send[2, half] = part[:HP].astype(BF16)
        p_mid[0, half] = part[HP:]
        part = route_part(xb, half)
        p_send[3, half] = part[HP:].astype(BF16)
        p_mid[1, half] = part[:HP]
    send(p_send.at[2], p_recv.at[2], r_ss.at[2], r_rs.at[2], dev_a)
    send(p_send.at[3], p_recv.at[3], r_ss.at[3], r_rs.at[3], dev_b)
    for half in range(2):
        p_own[half] = route_part(x, half)

    arrived(p_recv.at[0], r_ss.at[0], r_rs.at[0])
    p_send[5] = (p_mid[1] + p_recv[0].astype(F32)).astype(BF16)
    send(p_send.at[5], p_recv.at[5], r_ss.at[5], r_rs.at[5], dev_b)
    arrived(p_recv.at[1], r_ss.at[1], r_rs.at[1])
    p_send[4] = (p_mid[0] + p_recv[1].astype(F32)).astype(BF16)
    send(p_send.at[4], p_recv.at[4], r_ss.at[4], r_rs.at[4], dev_a)

    arrived(z_mid.at[pl.ds(0, HR)], t_ss.at[0], t_rs.at[0])
    send(z_mid.at[pl.ds(0, HR)], z_recv.at[pl.ds(0, HR)], t_ss.at[2], t_rs.at[2], dev_up)
    arrived(z_mid.at[pl.ds(HR, HR)], t_ss.at[1], t_rs.at[1])
    send(z_mid.at[pl.ds(HR, HR)], z_recv.at[pl.ds(HR, HR)], t_ss.at[3], t_rs.at[3], dev_dn)

    for i in range(2, 6):
        arrived(p_recv.at[i], r_ss.at[i], r_rs.at[i])
    first = p_own[:, :HP, :] + p_recv[2].astype(F32) + p_recv[5].astype(F32)
    second = p_own[:, HP:, :] + p_recv[3].astype(F32) + p_recv[4].astype(F32)
    rbuf[:, :4] = first.astype(BF16).reshape(2, 4, 16, FB)
    rbuf[:, 4:] = second.astype(BF16).reshape(2, 4, 16, FB)

    order = [8, 7, 9, 6, 10, 5, 11, 4, 12, 3, 13, 2, 14, 1, 15]
    for step in order:
        to = lax.rem(z + step, NZ)
        send(rbuf.at[lax.div(to, NL), lax.rem(to, NL)], dbuf.at[z], v_ss.at[step], v_rs.at[step], dev(x, y, to, c))
    dbuf[z] = rbuf[zh, zl]

    for i in range(2):
        part = pl.ds(i * HR, HR)
        arrived(z_recv.at[part], t_ss.at[2 + i], t_rs.at[2 + i])
    shared = s_own[zh] + z_recv[...].astype(F32)

    for step in order:
        frm = lax.rem(z + NZ - step, NZ)
        arrived(dbuf.at[frm], v_ss.at[step], v_rs.at[step])
    total = (dbuf[0:NL].astype(F32) + dbuf[NL:NZ].astype(F32)).astype(BF16)
    ysend[...] = dot(swap, total.reshape(ROWS, FB)).astype(BF16).reshape(NY, 16, FB)
    for r in range(1, NY):
        to = lax.rem(y + r, NY)
        send(ysend.at[to], ebuf.at[y], u_ss.at[r], u_rs.at[r], dev(x, to, z, c))
    ebuf[y] = ysend[y]
    for r in range(1, NY):
        frm = lax.rem(y + NY - r, NY)
        arrived(ebuf.at[frm], u_ss.at[r], u_rs.at[r])
    back = ebuf[...].reshape(ROWS, FB)
    out_ref[...] = (shared + dot(wcomb[0], back) + dot(wcomb[1], back)).astype(BF16)

    for copy in sends:
        copy.wait_send()


def local(
    tokens, expert_ids, combine_weight, old_plan, new_plan, gate_weight, up_weight, down_weight,
    shared_gate, shared_up, shared_down,
):
    dma = pltpu.SemaphoreType.DMA
    vmem = pltpu.VMEM
    return pl.pallas_call(
        kernel,
        out_shape=jax.ShapeDtypeStruct((TOK, FB), BF16),
        in_specs=[pl.BlockSpec(memory_space=pltpu.HBM)] * 11,
        out_specs=pl.BlockSpec(memory_space=pltpu.VMEM),
        scratch_shapes=[
            vmem((TOK, D), BF16),
            vmem((8, TOK), jnp.int32),
            vmem((8, TOK), F32),
            pltpu.SMEM((SLOTS,), jnp.int32),
            pltpu.SMEM((SLOTS,), jnp.int32),
            vmem((D, 2 * HB), BF16),
            vmem((D, 2 * HB), BF16),
            vmem((2, HB, D), BF16),
            vmem((2, HB, D), BF16),
            vmem((NY, 16, CH), BF16),
            vmem((NY, 16, CH), BF16),
            vmem((NL, 16, CH), BF16),
            vmem((2, NX, NL, 16, CH), BF16),
            vmem((2, ROWS, HB), BF16),
            vmem((2, TOK, HB), BF16),
            vmem((6, 2, TOK // 2, FB), BF16),
            vmem((6, 2, TOK // 2, FB), BF16),
            vmem((2, 2, TOK // 2, FB), F32),
            vmem((2, TOK, FB), F32),
            vmem((TOK, FB), BF16),
            vmem((TOK, FB), BF16),
            vmem((TOK, FB), BF16),
            vmem((2, ROWS, FB), F32),
            vmem((6, 2, ROWS // 2, FB), BF16),
            vmem((6, 2, ROWS // 2, FB), BF16),
            vmem((2, 2, ROWS // 2, FB), F32),
            vmem((2, NL, 16, FB), BF16),
            vmem((NZ, 16, FB), BF16),
            vmem((NY, 16, FB), BF16),
            vmem((NY, 16, FB), BF16),
            vmem((2, TOK, ROWS), BF16),
            dma((11,)),
            dma((8,)), dma((8,)),
            dma((7,)), dma((7,)),
            dma((9,)), dma((9,)),
            dma((6,)), dma((6,)),
            dma((6,)), dma((6,)),
            dma((6,)), dma((6,)),
            dma((16,)), dma((16,)),
            dma((4,)), dma((4,)),
            dma((8,)), dma((8,)),
        ],
        compiler_params=pltpu.CompilerParams(
            collective_id=0, has_side_effects=True, vmem_limit_bytes=60 * 2**20
        ),
        cost_estimate=pl.CostEstimate(flops=2 * 10**9, bytes_accessed=12 * 2**20, transcendentals=10**5),
    )(
        tokens, expert_ids.T, combine_weight.T, old_plan, new_plan, gate_weight, up_weight, down_weight,
        shared_gate, shared_up, shared_down,
    )


def solution(mesh):
    in_specs = (
        P("expert", None),
        P("expert", None),
        P("expert", None),
        P(),
        P(),
        P("expert", None, "dp"),
        P("expert", None, "dp"),
        P("expert", "dp", None),
        P(None, "dp"),
        P(None, "dp"),
        P("dp", None),
    )
    out_specs = P("expert", "dp")
    return jax.shard_map(local, mesh=mesh, in_specs=in_specs, out_specs=out_specs, check_vma=False)
```

time: 421 us -> 77.9 us (0.19)
  the two profiles are of different devices: /device:TPU:1 before, /device:TPU:2 now
where the time goes in v1:
time: 77.9 us; the launch traced here: 77.7 us
  Pallas kernels  76.1 us (98%)
  local copies, waits for them, and re-layouts  1.57 us (2%)
    pallas_call x1, Pallas kernels, local(): pl.pallas_call(kernel, out_shape=jax.ShapeDtypeStruct((TOK, FB), BF16), i...  76.1 us
    unnamed x1, local copies, waits for them, and re-layouts  1.57 us

profile of v1, /device:TPU:2, one launch (start us, length us, event | category | flops | bytes accessed | tf_op | source)
XLA Modules:
  0.0 77.7 jit_solution(14939480039578653942)
XLA Ops:
  0.0 76.1 %shard_map.109 = bf16[256,256]{1,0:T(8,128)(2,1)} custom-call(bf16[256,4096]{1,0:T(8,128)(2,1)} %tokens_in.1, s32[8,256]{1,0:T(8,128)} %bitcast.2, f32[8,256]{1,0:T(8,128)} %bitcast.3, s32[64]{0:T(128)} %old_in.1, s32[64]{0:T(128)} %new_in.1, bf16[1,4096,128]{2,1,0:T(8,128)(2,1)} %gate_in.1, bf16[1,4096,128]{2,1,0:T(8,128)(2,1)} %up_in.1, ...), custom_call_target="tpu_custom_call" | custom-call | flops 2000000000 | bytes 12582912 | tf_op jit(solution)/shard_map/pallas_call | solution.py:349
  76.2 1.6 %copy.13 = bf16[256,256]{1,0:T(8,128)(2,1)} copy(bf16[256,256]{1,0:T(8,128)(2,1)} %shard_map.109) | data formatting | bytes 262144

commit v2 on v1

v2 whole, which is shorter than its diff:
```python
import jax
import jax.numpy as jnp
from jax import lax
from jax.experimental import pallas as pl
from jax.experimental.pallas import tpu as pltpu
from jax.sharding import PartitionSpec as P

MESH = pl.DeviceIdType.MESH
BF16 = jnp.bfloat16
F32 = jnp.float32

NX, NY, NZ, NL = 4, 8, 16, 8
TOK = 256
D = 4096
HB = 128
SLOTS = 64
ROWS = 128
CH = 512
FB = 256


def dot(a, b):
    return jnp.dot(a, b, preferred_element_type=F32)


def gated(g, u):
    return (g / (1.0 + jnp.exp(-g)) * u).astype(BF16)


def kernel(
    tokens_in, ids_in, cw_in, old_in, new_in, gate_in, up_in, down_in, sgate_in, sup_in, sdown_in,
    out_ref,
    tokens, chunk, ids, cw, old, new, wgu, swgu, down, sdown,
    gbuf, abuf, bbuf, xrows, hid, shid,
    s_send, s_recv, s_mid, s_own, z_send, z_recv,
    p_own, p_send, p_recv, rbuf, dbuf, ysend, ebuf, wcomb,
    lsem, y_ss, y_rs, z_ss, z_rs, a_ss, a_rs, b_ss, b_rs, x_ss, x_rs, r_ss, r_rs, v_ss, v_rs,
    t_ss, t_rs, u_ss, u_rs,
):
    d = lax.axis_index("dp")
    e = lax.axis_index("expert")
    x = lax.div(d, 4)
    zh = lax.rem(lax.div(d, 2), 2)
    c = lax.rem(d, 2)
    y = lax.div(e, NL)
    zl = lax.rem(e, NL)
    z = zh * NL + zl
    xa = x + 1 - 2 * lax.rem(x, 2)
    xb = 3 - x
    xo = lax.rem(x + 2, NX)
    oc = 1 - c

    def dev(x_, y_, z_, c_):
        return (x_ * 4 + lax.div(z_, NL) * 2 + c_, y_ * NL + lax.rem(z_, NL))

    sib = dev(x, y, z, oc)
    dev_a = dev(xa, y, z, c)
    dev_b = dev(xb, y, z, c)
    dev_o = dev(xo, y, z, c)
    across = (dev_a, dev_b, dev_o)
    places = (xa, xb, xo)

    def load(src, dst, i):
        copy = pltpu.make_async_copy(src, dst, lsem.at[i])
        copy.start()
        return copy

    l_old = load(old_in, old, 0)
    l_new = load(new_in, new, 1)
    l_ids = load(ids_in, ids, 2)
    l_cw = load(cw_in, cw, 3)
    l_chunk = load(tokens_in.at[:, pl.ds(pl.multiple_of(x * 1024 + c * CH, CH), CH)], chunk, 4)
    l_sg = load(sgate_in, swgu.at[:, pl.ds(0, HB)], 5)
    l_su = load(sup_in, swgu.at[:, pl.ds(HB, HB)], 6)
    l_tok = load(tokens_in, tokens, 7)

    barrier = pltpu.get_barrier_semaphore()
    peers = [sib, dev_a, dev_b, dev_o]
    peers += [dev(x, lax.rem(y + r, NY), z, c) for r in range(1, NY)]
    peers += [dev(x, y, lax.rem(z + r, NZ), c) for r in range(1, NZ)]
    for peer in peers:
        pl.semaphore_signal(barrier, inc=1, device_id=peer, device_id_type=MESH)

    sends = []

    def send(src, dst, ss, rs, peer):
        copy = pltpu.make_async_remote_copy(
            src_ref=src, dst_ref=dst, send_sem=ss, recv_sem=rs, device_id=peer, device_id_type=MESH
        )
        copy.start()
        sends.append(copy)

    def arrived(dst, ss, rs):
        pltpu.make_async_remote_copy(
            src_ref=dst, dst_ref=dst, send_sem=ss, recv_sem=rs, device_id=sib, device_id_type=MESH
        ).wait_recv()

    l_old.wait()
    l_new.wait()
    lane8 = lax.broadcasted_iota(jnp.int32, (8, ROWS), 1)
    slot8 = lax.div(lane8, 2)

    held = jnp.full((8, ROWS), -1, jnp.int32)
    for s in range(SLOTS):
        held = jnp.where(slot8 == s, old[s], held)
    kept = jnp.zeros((8, ROWS), jnp.bool_)
    for s in range(SLOTS):
        kept = kept | (held == new[s])
    held = jnp.where(kept, held, -1).astype(F32)[0:1, :]
    held = jnp.transpose(jnp.broadcast_to(held, (ROWS, ROWS))).astype(jnp.int32)
    held = jnp.concatenate([held, held], axis=1)
    l_ids.wait()
    l_cw.wait()
    match = jnp.zeros((ROWS, TOK), F32)
    weight = jnp.zeros((ROWS, TOK), F32)
    for k in range(8):
        hit = ids[k : k + 1, :] == held
        match = match + jnp.where(hit, 1.0, 0.0)
        weight = weight + jnp.where(hit, cw[k : k + 1, :], 0.0)
    upper = jnp.where(
        lax.broadcasted_iota(jnp.int32, (TOK, TOK), 0) < lax.broadcasted_iota(jnp.int32, (TOK, TOK), 1),
        1.0, 0.0,
    ).astype(BF16)
    before = dot(match.astype(BF16), upper)
    place = lax.rem(lax.broadcasted_iota(jnp.int32, (ROWS, TOK), 0), 2).astype(F32)
    here = jnp.where(before == place, 1.0, 0.0)
    pick = (match * here).astype(BF16)
    weight = weight * here
    row = lax.broadcasted_iota(jnp.int32, (ROWS, ROWS), 0)
    col = lax.broadcasted_iota(jnp.int32, (ROWS, ROWS), 1)
    swapped = lax.rem(lax.div(row, 2), 8) * 16 + lax.div(row, 16) * 2 + lax.rem(row, 2)
    swap = jnp.where(col == swapped, 1.0, 0.0).astype(BF16)

    l_chunk.wait()
    for f in range(2):
        gbuf[f] = dot(pick, chunk[:, f * FB : (f + 1) * FB]).astype(BF16).reshape(NY, 16, FB)
        abuf[f, y] = gbuf[f, y]
        if f == 0:
            pl.semaphore_wait(barrier, len(peers))
        for r in range(1, NY):
            to = lax.rem(y + r, NY)
            send(gbuf.at[f, to], abuf.at[f, y], y_ss.at[f, r], y_rs.at[f, r], dev(x, to, z, c))
    l_sd = load(sdown_in, sdown.at[c], 8)
    send(sdown_in, sdown.at[c], a_ss.at[0], a_rs.at[0], sib)
    l_g = load(gate_in.at[0], wgu.at[:, pl.ds(0, HB)], 9)
    l_u = load(up_in.at[0], wgu.at[:, pl.ds(HB, HB)], 10)

    weight = jnp.transpose(weight)
    high = weight.astype(BF16)
    wcomb[0] = high
    wcomb[1] = (weight - high.astype(F32)).astype(BF16)

    l_sg.wait()
    l_su.wait()
    l_tok.wait()
    both = dot(tokens[...], swgu[...])
    shid[c] = gated(both[:, :HB], both[:, HB:])
    send(shid.at[c], shid.at[c], a_ss.at[2], a_rs.at[2], sib)

    steps = [1, 15, 2, 14, 3, 13, 4 + 8 * c]
    for f in range(2):
        for r in range(1, NY):
            frm = lax.rem(y + NY - r, NY)
            arrived(abuf.at[f, frm], y_ss.at[f, r], y_rs.at[f, r])
        bbuf[f] = dot(swap, abuf[f].reshape(ROWS, FB)).astype(BF16).reshape(NL, 16, FB)
        for i, step in enumerate(steps):
            to = lax.rem(z + step, NZ)
            send(bbuf.at[f, lax.rem(to, NL)], xrows.at[c, x, f, zl], z_ss.at[f, i], z_rs.at[f, i], dev(x, y, to, c))
        xrows[c, x, f, zl] = bbuf[f, zl]
    l_d = load(down_in.at[0], down.at[c], 11)
    send(down_in.at[0], down.at[c], a_ss.at[1], a_rs.at[1], sib)

    l_sd.wait()
    arrived(sdown.at[oc], a_ss.at[0], a_rs.at[0])
    arrived(shid.at[oc], a_ss.at[2], a_rs.at[2])
    sh0 = shid[0]
    sh1 = shid[1]

    def columns(ref, core, x_, half):
        at = pl.multiple_of(x_ * 1024 + half * CH + c * FB, FB)
        return ref[core, :, pl.ds(at, FB)]

    def shared_part(x_, half):
        return dot(sh0, columns(sdown, 0, x_, half)) + dot(sh1, columns(sdown, 1, x_, half))

    HR = TOK // 2
    halves = (1 - zh, zh)

    def shared_first(k):
        part = shared_part(xo, halves[k]).astype(BF16)
        s_send[k, 0] = part[:HR]
        s_send[k, 1] = part[HR:]
        part = shared_part(xa, halves[k])
        s_send[k, 2] = part[:HR].astype(BF16)
        s_mid[k, 0] = part[HR:]
        part = shared_part(xb, halves[k])
        s_send[k, 3] = part[HR:].astype(BF16)
        s_mid[k, 1] = part[:HR]
        for i in range(4):
            send(s_send.at[k, i], s_recv.at[k, i], b_ss.at[k, i], b_rs.at[k, i], across[i % 2])
        s_own[k] = shared_part(x, halves[k])

    def shared_second(k):
        arrived(s_recv.at[k, 0], b_ss.at[k, 0], b_rs.at[k, 0])
        s_send[k, 5] = (s_mid[k, 1] + s_recv[k, 0].astype(F32)).astype(BF16)
        send(s_send.at[k, 5], s_recv.at[k, 5], b_ss.at[k, 5], b_rs.at[k, 5], dev_b)
        arrived(s_recv.at[k, 1], b_ss.at[k, 1], b_rs.at[k, 1])
        s_send[k, 4] = (s_mid[k, 0] + s_recv[k, 1].astype(F32)).astype(BF16)
        send(s_send.at[k, 4], s_recv.at[k, 4], b_ss.at[k, 4], b_rs.at[k, 4], dev_a)

    def shared_last(k):
        for i in range(2, 6):
            arrived(s_recv.at[k, i], b_ss.at[k, i], b_rs.at[k, i])
        s_own[k, :HR] = s_own[k, :HR] + s_recv[k, 2].astype(F32) + s_recv[k, 5].astype(F32)
        s_own[k, HR:] = s_own[k, HR:] + s_recv[k, 3].astype(F32) + s_recv[k, 4].astype(F32)

    shared_first(0)

    for f in range(2):
        for i, step in enumerate(steps):
            frm = lax.rem(z + NZ - step, NZ)
            arrived(xrows.at[c, x, f, lax.rem(frm, NL)], z_ss.at[f, i], z_rs.at[f, i])
        piece = xrows.at[c, x, f]
        for i in (2, 0, 1):
            send(piece, piece, x_ss.at[f, i], x_rs.at[f, i], across[i])
        send(piece, piece, a_ss.at[4 + f], a_rs.at[4 + f], sib)
        if f == 0:
            shared_second(0)

    l_g.wait()
    l_u.wait()

    def product(core, x_, f):
        at = pl.multiple_of(x_ * 1024 + core * CH + f * FB, FB)
        return dot(xrows[core, x_, f].reshape(ROWS, FB), wgu[pl.ds(at, FB), :])

    acc = product(c, x, 0) + product(c, x, 1)
    for f in range(2):
        for i in range(3):
            piece = xrows.at[c, places[i], f]
            arrived(piece, x_ss.at[f, i], x_rs.at[f, i])
            send(piece, piece, a_ss.at[6 + 3 * f + i], a_rs.at[6 + 3 * f + i], sib)
            acc = acc + product(c, places[i], f)
        if f == 0:
            shared_last(0)
            z_send[...] = s_own[0].astype(BF16)
            send(z_send, z_recv, t_ss.at[0], t_rs.at[0], dev(x, y, lax.rem(z + NL, NZ), c))
    shared_first(1)

    for f in range(2):
        arrived(xrows.at[oc, x, f], a_ss.at[4 + f], a_rs.at[4 + f])
        acc = acc + product(oc, x, f)
    for f in range(2):
        for i in range(3):
            arrived(xrows.at[oc, places[i], f], a_ss.at[6 + 3 * f + i], a_rs.at[6 + 3 * f + i])
            acc = acc + product(oc, places[i], f)
    hid[c] = gated(acc[:, :HB], acc[:, HB:])
    send(hid.at[c], hid.at[c], a_ss.at[3], a_rs.at[3], sib)

    l_d.wait()
    arrived(down.at[oc], a_ss.at[1], a_rs.at[1])
    arrived(hid.at[oc], a_ss.at[3], a_rs.at[3])
    h0 = hid[0]
    h1 = hid[1]

    def route_part(x_, half):
        return dot(h0, columns(down, 0, x_, half)) + dot(h1, columns(down, 1, x_, half))

    for k in range(2):
        half = halves[k]
        for i in (2, 0, 1):
            p_send[k, i] = route_part(places[i], half).astype(BF16)
            send(p_send.at[k, i], p_recv.at[k, i], r_ss.at[k, i], r_rs.at[k, i], across[i])
        p_own[k] = route_part(x, half)

    shared_second(1)
    for k in range(2):
        half = halves[k]
        total = p_own[k]
        for i in range(3):
            arrived(p_recv.at[k, i], r_ss.at[k, i], r_rs.at[k, i])
            total = total + p_recv[k, i].astype(F32)
        rbuf[k] = total.astype(BF16).reshape(NL, 16, FB)
        for r in range(k, NL):
            to = lax.rem(zl + r, NL)
            at = (1 - k) * NL + r
            send(rbuf.at[k, to], dbuf.at[z], v_ss.at[at], v_rs.at[at], dev(x, y, half * NL + to, c))
    dbuf[z] = rbuf[1, zl]

    shared_last(1)
    arrived(z_recv, t_ss.at[0], t_rs.at[0])
    shared = s_own[1] + z_recv[...].astype(F32)

    for k in range(2):
        half = halves[k]
        for r in range(k, NL):
            frm = half * NL + lax.rem(zl + NL - r, NL)
            at = (1 - k) * NL + r
            arrived(dbuf.at[frm], v_ss.at[at], v_rs.at[at])
    total = (dbuf[0:NL].astype(F32) + dbuf[NL:NZ].astype(F32)).astype(BF16)
    ysend[...] = dot(swap, total.reshape(ROWS, FB)).astype(BF16).reshape(NY, 16, FB)
    for r in range(1, NY):
        to = lax.rem(y + r, NY)
        send(ysend.at[to], ebuf.at[y], u_ss.at[r], u_rs.at[r], dev(x, to, z, c))
    ebuf[y] = ysend[y]
    for r in range(1, NY):
        frm = lax.rem(y + NY - r, NY)
        arrived(ebuf.at[frm], u_ss.at[r], u_rs.at[r])
    back = ebuf[...].reshape(ROWS, FB)
    out_ref[...] = (shared + dot(wcomb[0], back) + dot(wcomb[1], back)).astype(BF16)

    for copy in sends:
        copy.wait_send()


def local(
    tokens, expert_ids, combine_weight, old_plan, new_plan, gate_weight, up_weight, down_weight,
    shared_gate, shared_up, shared_down,
):
    dma = pltpu.SemaphoreType.DMA
    vmem = pltpu.VMEM
    return pl.pallas_call(
        kernel,
        out_shape=jax.ShapeDtypeStruct((TOK, FB), BF16),
        in_specs=[pl.BlockSpec(memory_space=pltpu.HBM)] * 11,
        out_specs=pl.BlockSpec(memory_space=pltpu.VMEM),
        scratch_shapes=[
            vmem((TOK, D), BF16),
            vmem((TOK, CH), BF16),
            vmem((8, TOK), jnp.int32),
            vmem((8, TOK), F32),
            pltpu.SMEM((SLOTS,), jnp.int32),
            pltpu.SMEM((SLOTS,), jnp.int32),
            vmem((D, 2 * HB), BF16),
            vmem((D, 2 * HB), BF16),
            vmem((2, HB, D), BF16),
            vmem((2, HB, D), BF16),
            vmem((2, NY, 16, FB), BF16),
            vmem((2, NY, 16, FB), BF16),
            vmem((2, NL, 16, FB), BF16),
            vmem((2, NX, 2, NL, 16, FB), BF16),
            vmem((2, ROWS, HB), BF16),
            vmem((2, TOK, HB), BF16),
            vmem((2, 6, TOK // 2, FB), BF16),
            vmem((2, 6, TOK // 2, FB), BF16),
            vmem((2, 2, TOK // 2, FB), F32),
            vmem((2, TOK, FB), F32),
            vmem((TOK, FB), BF16),
            vmem((TOK, FB), BF16),
            vmem((2, ROWS, FB), F32),
            vmem((2, 3, ROWS, FB), BF16),
            vmem((2, 3, ROWS, FB), BF16),
            vmem((2, NL, 16, FB), BF16),
            vmem((NZ, 16, FB), BF16),
            vmem((NY, 16, FB), BF16),
            vmem((NY, 16, FB), BF16),
            vmem((2, TOK, ROWS), BF16),
            dma((12,)),
            dma((2, 8)), dma((2, 8)),
            dma((2, 7)), dma((2, 7)),
            dma((12,)), dma((12,)),
            dma((2, 6)), dma((2, 6)),
            dma((2, 3)), dma((2, 3)),
            dma((2, 3)), dma((2, 3)),
            dma((16,)), dma((16,)),
            dma((1,)), dma((1,)),
            dma((8,)), dma((8,)),
        ],
        compiler_params=pltpu.CompilerParams(
            collective_id=0, has_side_effects=True, vmem_limit_bytes=60 * 2**20
        ),
        cost_estimate=pl.CostEstimate(flops=2 * 10**9, bytes_accessed=12 * 2**20, transcendentals=10**5),
    )(
        tokens, expert_ids.T, combine_weight.T, old_plan, new_plan, gate_weight, up_weight, down_weight,
        shared_gate, shared_up, shared_down,
    )


def solution(mesh):
    in_specs = (
        P("expert", None),
        P("expert", None),
        P("expert", None),
        P(),
        P(),
        P("expert", None, "dp"),
        P("expert", None, "dp"),
        P("expert", "dp", None),
        P(None, "dp"),
        P(None, "dp"),
        P("dp", None),
    )
    out_specs = P("expert", "dp")
    return jax.shard_map(local, mesh=mesh, in_specs=in_specs, out_specs=out_specs, check_vma=False)
```

time: 77.9 us -> 68 us (0.87)
  the two profiles are of different devices: /device:TPU:2 before, /device:TPU:8 now
where the time goes in v2:
time: 68 us; the launch traced here: 67.8 us
  Pallas kernels  66.2 us (97%)
  local copies, waits for them, and re-layouts  1.57 us (2%)
    pallas_call x1, Pallas kernels, local(): pl.pallas_call(kernel, out_shape=jax.ShapeDtypeStruct((TOK, FB), BF16), i...  66.2 us
    unnamed x1, local copies, waits for them, and re-layouts  1.57 us

profile of v2, /device:TPU:8, one launch (start us, length us, event | category | flops | bytes accessed | tf_op | source)
XLA Modules:
  0.0 67.8 jit_solution(5317562360197274840)
XLA Ops:
  0.0 66.2 %shard_map.109 = bf16[256,256]{1,0:T(8,128)(2,1)} custom-call(bf16[256,4096]{1,0:T(8,128)(2,1)} %tokens_in.1, s32[8,256]{1,0:T(8,128)} %bitcast.2, f32[8,256]{1,0:T(8,128)} %bitcast.3, s32[64]{0:T(128)} %old_in.1, s32[64]{0:T(128)} %new_in.1, bf16[1,4096,128]{2,1,0:T(8,128)(2,1)} %gate_in.1, bf16[1,4096,128]{2,1,0:T(8,128)(2,1)} %up_in.1, ...), custom_call_target="tpu_custom_call" | custom-call | flops 2000000000 | bytes 12582912 | tf_op jit(solution)/shard_map/pallas_call | solution.py:322
  66.2 1.6 %copy.13 = bf16[256,256]{1,0:T(8,128)(2,1)} copy(bf16[256,256]{1,0:T(8,128)(2,1)} %shard_map.109) | data formatting | bytes 262144

commit v3 on v2

--- a/solution.py
+++ b/solution.py
@@ -70,9 +70,6 @@
     l_ids = load(ids_in, ids, 2)
     l_cw = load(cw_in, cw, 3)
     l_chunk = load(tokens_in.at[:, pl.ds(pl.multiple_of(x * 1024 + c * CH, CH), CH)], chunk, 4)
-    l_sg = load(sgate_in, swgu.at[:, pl.ds(0, HB)], 5)
-    l_su = load(sup_in, swgu.at[:, pl.ds(HB, HB)], 6)
-    l_tok = load(tokens_in, tokens, 7)
 
     barrier = pltpu.get_barrier_semaphore()
     peers = [sib, dev_a, dev_b, dev_o]
@@ -80,6 +77,10 @@
     peers += [dev(x, y, lax.rem(z + r, NZ), c) for r in range(1, NZ)]
     for peer in peers:
         pl.semaphore_signal(barrier, inc=1, device_id=peer, device_id_type=MESH)
+
+    l_sg = load(sgate_in, swgu.at[:, pl.ds(0, HB)], 5)
+    l_su = load(sup_in, swgu.at[:, pl.ds(HB, HB)], 6)
+    l_tok = load(tokens_in, tokens, 7)
 
     sends = []
 

time: 68 us -> 67.9 us (level)
  no operation moved by 1% of the time
where the time goes in v3:
time: 67.9 us; the launch traced here: 67.8 us
  Pallas kernels  66.2 us (97%)
  local copies, waits for them, and re-layouts  1.57 us (2%)
    pallas_call x1, Pallas kernels, local(): pl.pallas_call(kernel, out_shape=jax.ShapeDtypeStruct((TOK, FB), BF16), i...  66.2 us
    unnamed x1, local copies, waits for them, and re-layouts  1.57 us

profile of v3, /device:TPU:8, one launch (start us, length us, event | category | flops | bytes accessed | tf_op | source)
XLA Modules:
  0.0 67.8 jit_solution(14816302287840426528)
XLA Ops:
  0.0 66.2 %shard_map.109 = bf16[256,256]{1,0:T(8,128)(2,1)} custom-call(bf16[256,4096]{1,0:T(8,128)(2,1)} %tokens_in.1, s32[8,256]{1,0:T(8,128)} %bitcast.2, f32[8,256]{1,0:T(8,128)} %bitcast.3, s32[64]{0:T(128)} %old_in.1, s32[64]{0:T(128)} %new_in.1, bf16[1,4096,128]{2,1,0:T(8,128)(2,1)} %gate_in.1, bf16[1,4096,128]{2,1,0:T(8,128)(2,1)} %up_in.1, ...), custom_call_target="tpu_custom_call" | custom-call | flops 2000000000 | bytes 12582912 | tf_op jit(solution)/shard_map/pallas_call | solution.py:323
  66.2 1.6 %copy.13 = bf16[256,256]{1,0:T(8,128)(2,1)} copy(bf16[256,256]{1,0:T(8,128)(2,1)} %shard_map.109) | data formatting | bytes 262144
